TPU v7x, 256 devices: a whole 4x4x8 slice. The times are simulated.
256 devices in a mesh: qa: 8 (over y_lo, x), qb: 32 (over y_hi, z, core).
Axes of the slice: x: 4, y: 4 (y_hi: 2, y_lo: 2; y = y_hi * 2 + y_lo), z: 8, core: 2. Of those that a mesh axis runs over, the one named last changes fastest.
Arguments:
- amplitudes: float32 [2, 16777216], P(None, ('qa', 'qb')), may hold values from -6 to 6
- gate_blocks: float32 [4, 6, 2, 128, 128], replicated, may hold values from -0.375 to 0.375
- phase_low: float32 [4, 256], replicated, may hold values from -3.140625 to 3.140625
- phase_high: float32 [4, 256], replicated, may hold values from -3.140625 to 3.140625
- phase_global: float32 [4, 8, 32], P(None, 'qa', 'qb'), may hold values from -3.140625 to 3.140625
Outputs:
- final_state: float32 [2, 16777216], P(None, ('qa', 'qb'))
All inputs are finite; a program needn't handle non-finite values.
Results may differ from a plain program's by a relative error of at most 0.00011.
Values sent between devices are 32-bit elements; how exact they have to be, the bound alone decides.
A program may use at most 64 MiB of HBM per device.

v0:
```python
import jax
import jax.numpy as jnp
from jax import lax
from jax.sharding import PartitionSpec as P


def apply_gate(state, matrix, where):
    width = matrix.shape[-1]
    cells = state.shape[2]
    stacked = jnp.concatenate([matrix[0], matrix[1]], axis=0)
    if where == 0:
        values = state.reshape(2 * (cells // width), width)
        product = lax.dot_general(
            values, stacked, (((1,), (1,)), ((), ())), precision=lax.Precision.HIGHEST
        )
        product = product.reshape(2, cells // width, 2, width)
        out_real = product[0, :, 0] - product[1, :, 1]
        out_imag = product[0, :, 1] + product[1, :, 0]
    elif where == 1:
        upper = cells // (width * width)
        values = state.reshape(2, upper, width, width)
        product = lax.dot_general(
            stacked, values, (((1,), (2,)), ((), ())), precision=lax.Precision.HIGHEST
        )
        product = product.reshape(2, width, 2, upper, width)
        out_real = jnp.transpose(product[0, :, 0] - product[1, :, 1], (1, 0, 2))
        out_imag = jnp.transpose(product[1, :, 0] + product[0, :, 1], (1, 0, 2))
    else:
        values = state.reshape(2, width, cells // width)
        product = lax.dot_general(
            stacked, values, (((1,), (1,)), ((), ())), precision=lax.Precision.HIGHEST
        )
        product = product.reshape(2, width, 2, cells // width)
        out_real = product[0, :, 0] - product[1, :, 1]
        out_imag = product[1, :, 0] + product[0, :, 1]
    return jnp.stack([out_real.reshape(cells), out_imag.reshape(cells)]).reshape(2, 1, cells)


def apply_phase(state, low_angles, high_angles, global_angles):
    local = (high_angles[:, None] + low_angles[None, :]).reshape(-1)
    theta = global_angles.reshape(-1, 1) + local[None, :]
    cosine = jnp.cos(theta)
    sine = jnp.sin(theta)
    return jnp.stack([state[0] * cosine - state[1] * sine, state[0] * sine + state[1] * cosine])


def regroup_with_gate(state, which, matrix):
    cells = state.shape[2]
    width = matrix.shape[-1]

    def lowest_gate(pieces):
        shape = pieces.shape
        flat = pieces.reshape(2, 1, shape[1] * shape[2] * shape[3])
        return apply_gate(flat, matrix, 0).reshape(shape)

    if which == 0:
        count = lax.axis_size("qa")
        blocks = state.reshape(2, count, cells // (count * width), width)
        moved = lowest_gate(lax.all_to_all(blocks, "qa", split_axis=1, concat_axis=1, tiled=True))
    else:
        count = lax.axis_size("qb")
        blocks = state.reshape(2, count, cells // (count * width), width)
        moved = lowest_gate(lax.all_to_all(blocks, "qb", split_axis=1, concat_axis=1, tiled=True))
    return moved.reshape(2, 1, cells)


def body(amplitudes, gate_blocks, phase_low, phase_high, phase_global):
    cells = amplitudes.shape[1]
    state = amplitudes.reshape(2, 1, cells)
    segments = gate_blocks.shape[0]
    per_segment = gate_blocks.shape[1]
    done_lowest = False
    for segment in range(segments):
        for gate in range(per_segment):
            if gate == 0 and done_lowest:
                continue
            state = apply_gate(state, gate_blocks[segment, gate], gate % 3)
        done_lowest = False
        state = apply_phase(
            state, phase_low[segment], phase_high[segment], phase_global[segment].reshape(1)
        )
        if segment < 3:
            which = 1 if segment == 1 else 0
            state = regroup_with_gate(state, which, gate_blocks[segment + 1, 0])
            done_lowest = True
    return state.reshape(2, cells)


def solution(mesh):
    return jax.shard_map(
        body,
        mesh=mesh,
        in_specs=(P(None, ("qa", "qb")), P(), P(), P(), P(None, "qa", "qb")),
        out_specs=P(None, ("qa", "qb")),
        check_vma=False,
    )
```

profile of v0, /device:TPU:32, one launch (start us, length us, event | category | flops | bytes accessed | tf_op | source)
XLA Modules:
  0.0 105.7 jit_solution(10410167867592833478)
XLA Ops:
  0.0 2.2 %slice_bitcast_fusion.3 = (f32[128,128]{1,0:T(8,128)S(1)}, f32[128,128]{1,0:T(8,128)S(1)}, f32[128,128]{1,0:T(8,128)S(1)}, f32[128,128]{1,0:T(8,128)S(1)}, f32[1...) fusion(f32[4,6,2,128,128]{4,3,2,1,0:T(8,128)} %param.6), kind=kLoop, calls=%fused_computation.214 | loop fusion | bytes 2490368 | tf_op jit(solution)/shard_map/squeeze | solution.py:10
  2.2 2.1 %slice_bitcast_fusion.21 = (f32[128,128]{1,0:T(8,128)}, f32[128,128]{1,0:T(8,128)}, f32[128,128]{1,0:T(8,128)}, f32[128,128]{1,0:T(8,128)S(1)}, f32[128,128]{1,0...) fusion(f32[4,6,2,128,128]{4,3,2,1,0:T(8,128)} %param.6), kind=kLoop, calls=%fused_computation.232 | loop fusion | bytes 2490368 | tf_op jit(solution)/shard_map/squeeze | solution.py:10
  4.8 1.9 %convolution_bitcast_fusion = f32[1024,256]{0,1:T(8,128)S(1)} fusion(f32[1024,128]{1,0:T(8,128)S(1)} %reshape_reshape.2, f32[128,128]{1,0:T(8,128)} %get-tuple-element.20, f32[128,128]{1,0:T(8,128)} %get-tuple-element.21), kind=kOutput, calls=%fused_computation | convolution fusion | flops 402685952 | bytes 1703936 | tf_op jit(solution)/shard_map/dot_general | solution.py:13
  10.5 1.0 fusion.3
  11.8 1.0 fusion.6
  12.9 1.0 fusion.9
  14.1 1.0 fusion.12
  16.2 1.8 %fusion.82 = (f32[1,8,64,128]{3,2,0,1:T(8,128)S(1)}, f32[1,8,64,128]{3,2,0,1:T(8,128)S(1)}) fusion(f32[1,8,64,128]{3,2,1,0:T(8,128)S(1)} %add.638, f32[1,8,64,128]{3,2,1,0:T(8,128)S(1)} %sub.368, f32[64,128]{1,0:T(8,128)S(1)} %bitcast.579, f32[8,64]{1,0:T(8,128)S(1)} %copy.27, f32[]{:T(128)} %bitcast.106), kind=kLoop, calls=%fused_computation.169 | loop fusion | flops 524288 | bytes 1083396 | tf_op jit(solution)/shard_map/sub | solution.py:44
  18.9 5.3 %all-to-all-start = ((f32[2,8,64,128]{3,2,0,1:T(8,128)}), f32[2,8,64,128]{3,2,0,1:T(8,128)S(1)}, u32[]{:S(2)}, u32[]{:S(2)}) async-start(f32[2,8,64,128]{3,2,0,1:T(8,128)} %pad_maximum_fusion), calls=%async_computation | async-start | bytes 1048576 | tf_op jit(solution)/shard_map/all_to_all | solution.py:59
  24.5 9.7 %all-to-all-done = f32[2,8,64,128]{3,2,0,1:T(8,128)S(1)} async-done(((f32[2,8,64,128]{3,2,0,1:T(8,128)}), f32[2,8,64,128]{3,2,0,1:T(8,128)S(1)}, u32[]{:S(2)}, u32[]{:S(2)}) %all-to-all-start) | async-done | bytes 524320 | tf_op jit(solution)/shard_map/all_to_all | solution.py:59
  34.3 1.0 fusion.118
  35.4 1.0 fusion.15
  36.5 1.0 fusion.18
  37.7 1.0 fusion.21
  39.9 1.0 fusion.27
  41.0 1.7 %fusion.80 = (f32[1,32,16,128]{3,2,0,1:T(8,128)S(1)}, f32[1,32,16,128]{3,2,0,1:T(8,128)S(1)}) fusion(f32[1,32,16,128]{3,2,1,0:T(8,128)S(1)} %add.663, f32[1,32,16,128]{3,2,1,0:T(8,128)S(1)} %sub.381, f32[16,128]{1,0:T(8,128)S(1)} %bitcast.582, f32[32,16]{1,0:T(8,128)S(1)} %copy.34, f32[]{:T(128)} %bitcast.143), kind=kLoop, calls=%fused_computation.163 | loop fusion | flops 524288 | bytes 1058820 | tf_op jit(solution)/shard_map/sub | solution.py:44
  43.6 11.1 %all-to-all-start.1 = ((f32[2,32,16,128]{3,2,0,1:T(8,128)}), f32[2,32,16,128]{3,2,0,1:T(8,128)S(1)}, u32[]{:S(2)}, u32[]{:S(2)}) async-start(f32[2,32,16,128]{3,2,0,1:T(8,128)} %pad_maximum_fusion.1), calls=%async_computation.1 | async-start | bytes 1048576 | tf_op jit(solution)/shard_map/all_to_all | solution.py:63
  54.9 1.6 %fusion.84 = (f32[256,256]{1,0:T(8,128)S(1)}, f32[256,256]{1,0:T(8,128)S(1)}) fusion(f32[256]{0:T(256)S(1)} %bitcast.585, f32[256]{0:T(256)S(1)} %bitcast.584, f32[]{:T(128)} %bitcast.217), kind=kLoop, calls=%fused_computation.174 | loop fusion | flops 131072 | bytes 526340 | tf_op jit(solution)/shard_map/sin | solution.py:43
  57.2 1.2 %slice_bitcast_fusion.41 = (f32[128,128]{1,0:T(8,128)S(1)}, f32[128,128]{1,0:T(8,128)S(1)}, f32[128,128]{1,0:T(8,128)S(1)}, f32[128,128]{1,0:T(8,128)S(1)}, f32[...) fusion(f32[4,6,2,128,128]{4,3,2,1,0:T(8,128)} %param.6), kind=kLoop, calls=%fused_computation.252 | loop fusion | bytes 1310720 | tf_op jit(solution)/shard_map/squeeze | solution.py:10
  58.3 15.6 %all-to-all-done.1 = f32[2,32,16,128]{3,2,0,1:T(8,128)S(1)} async-done(((f32[2,32,16,128]{3,2,0,1:T(8,128)}), f32[2,32,16,128]{3,2,0,1:T(8,128)S(1)}, u32[]{:S(2)}, u32[]{:S(2)}) %all-to-all-start.1) | async-done | bytes 524320 | tf_op jit(solution)/shard_map/all_to_all | solution.py:63
  73.9 1.0 fusion.119
  75.0 1.0 fusion.30
  77.3 1.0 fusion.36
  79.5 1.0 fusion.42
  80.6 1.9 %fusion.78 = (f32[1,8,64,128]{3,2,0,1:T(8,128)S(1)}, f32[1,8,64,128]{3,2,0,1:T(8,128)S(1)}) fusion(f32[1,8,64,128]{3,2,1,0:T(8,128)S(1)} %add.688, f32[1,8,64,128]{3,2,1,0:T(8,128)S(1)} %sub.394, f32[64,128]{1,0:T(8,128)S(1)} %bitcast.578, f32[8,64]{1,0:T(8,128)S(1)} %copy.41, f32[]{:T(128)} %bitcast.180), kind=kLoop, calls=%fused_computation.157 | loop fusion | flops 524288 | bytes 1083396 | tf_op jit(solution)/shard_map/sub | solution.py:44
  83.3 3.8 %all-to-all-start.2 = ((f32[2,8,64,128]{3,2,0,1:T(8,128)}), f32[2,8,64,128]{3,2,0,1:T(8,128)S(1)}, u32[]{:S(2)}, u32[]{:S(2)}) async-start(f32[2,8,64,128]{3,2,0,1:T(8,128)} %pad_maximum_fusion.2), calls=%async_computation.2 | async-start | bytes 1048576 | tf_op jit(solution)/shard_map/all_to_all | solution.py:59
  87.2 9.3 %all-to-all-done.2 = f32[2,8,64,128]{3,2,0,1:T(8,128)S(1)} async-done(((f32[2,8,64,128]{3,2,0,1:T(8,128)}), f32[2,8,64,128]{3,2,0,1:T(8,128)S(1)}, u32[]{:S(2)}, u32[]{:S(2)}) %all-to-all-start.2) | async-done | bytes 524320 | tf_op jit(solution)/shard_map/all_to_all | solution.py:59
  96.6 1.0 fusion.120
  97.6 1.0 fusion.45
  99.9 1.0 fusion.51
  101.0 1.0 fusion.54
  104.4 1.3 %maximum_bitcast_fusion.40 = f32[2,65536]{1,0:T(2,128)} fusion(f32[1,1,65536]{2,0,1:T(1,128)S(1)} %get-tuple-element.57, f32[1,1,65536]{2,0,1:T(1,128)S(1)} %get-tuple-element.56), kind=kLoop, calls=%fused_computation.84 | loop fusion | flops 131072 | bytes 1048576 | tf_op jit(solution)/shard_map/reshape | solution.py:86
  (135 shorter events, 17.4 us)
Async XLA Ops:
  0.0 4.3 %copy-start = (f32[2,65536]{1,0:T(2,128)S(1)}, f32[2,65536]{1,0:T(2,128)}, u32[]{:S(2)}) copy-start(f32[2,65536]{1,0:T(2,128)} %param.5) | copy-start | bytes 1572868
  10.3 1.4 %copy-start.7 = (f32[128,128]{1,0:T(8,128)S(1)}, f32[128,128]{1,0:T(8,128)}, u32[]{:S(2)}) copy-start(f32[128,128]{1,0:T(8,128)} %get-tuple-element.14) | copy-start | bytes 196612
  10.3 1.4 %copy-start.8 = (f32[128,128]{1,0:T(8,128)S(1)}, f32[128,128]{1,0:T(8,128)}, u32[]{:S(2)}) copy-start(f32[128,128]{1,0:T(8,128)} %get-tuple-element.15) | copy-start | bytes 196612
  10.3 1.4 %copy-start.9 = (f32[128,128]{1,0:T(8,128)S(1)}, f32[128,128]{1,0:T(8,128)}, u32[]{:S(2)}) copy-start(f32[128,128]{1,0:T(8,128)} %get-tuple-element.18) | copy-start | bytes 196612
  10.4 1.4 %copy-start.10 = (f32[128,128]{1,0:T(8,128)S(1)}, f32[128,128]{1,0:T(8,128)}, u32[]{:S(2)}) copy-start(f32[128,128]{1,0:T(8,128)} %get-tuple-element.19) | copy-start | bytes 196612
  11.5 1.3 %copy-start.3 = (f32[128,128]{1,0:T(8,128)S(1)}, f32[128,128]{1,0:T(8,128)}, u32[]{:S(2)}) copy-start(f32[128,128]{1,0:T(8,128)} %get-tuple-element.26) | copy-start | bytes 196612
  11.5 1.3 %copy-start.4 = (f32[128,128]{1,0:T(8,128)S(1)}, f32[128,128]{1,0:T(8,128)}, u32[]{:S(2)}) copy-start(f32[128,128]{1,0:T(8,128)} %get-tuple-element.27) | copy-start | bytes 196612
  11.5 1.3 %copy-start.5 = (f32[128,128]{1,0:T(8,128)S(1)}, f32[128,128]{1,0:T(8,128)}, u32[]{:S(2)}) copy-start(f32[128,128]{1,0:T(8,128)} %get-tuple-element.28) | copy-start | bytes 196612
  11.5 1.3 %copy-start.6 = (f32[128,128]{1,0:T(8,128)S(1)}, f32[128,128]{1,0:T(8,128)}, u32[]{:S(2)}) copy-start(f32[128,128]{1,0:T(8,128)} %get-tuple-element.29) | copy-start | bytes 196612
  13.9 1.4 %copy-start.12 = (f32[4,256]{1,0:T(4,128)S(1)}, f32[4,256]{1,0:T(4,128)}, u32[]{:S(2)}) copy-start(f32[4,256]{1,0:T(4,128)} %param.8) | copy-start | bytes 12292
  14.0 1.5 %copy-start.13 = (f32[4,256]{1,0:T(4,128)S(1)}, f32[4,256]{1,0:T(4,128)}, u32[]{:S(2)}) copy-start(f32[4,256]{1,0:T(4,128)} %param.7) | copy-start | bytes 12292
  14.0 1.5 %copy-start.11 = (f32[4,1,1]{0,2,1:T(1,128)S(1)}, f32[4,1,1]{0,2,1:T(1,128)}, u32[]{:S(2)}) copy-start(f32[4,1,1]{0,2,1:T(1,128)} %param.9) | copy-start | bytes 52
  15.1 9.4 %copy-start.1 = (f32[128,128]{1,0:T(8,128)S(1)}, f32[128,128]{1,0:T(8,128)}, u32[]{:S(2)}) copy-start(f32[128,128]{1,0:T(8,128)} %get-tuple-element.32) | copy-start | bytes 196612
  15.1 9.4 %copy-start.2 = (f32[128,128]{1,0:T(8,128)S(1)}, f32[128,128]{1,0:T(8,128)}, u32[]{:S(2)}) copy-start(f32[128,128]{1,0:T(8,128)} %get-tuple-element.33) | copy-start | bytes 196612
  18.9 15.4 %all-to-all-start = ((f32[2,8,64,128]{3,2,0,1:T(8,128)}), f32[2,8,64,128]{3,2,0,1:T(8,128)S(1)}, u32[]{:S(2)}, u32[]{:S(2)}) async-start(f32[2,8,64,128]{3,2,0,1:T(8,128)} %pad_maximum_fusion), calls=%async_computation | async-start | bytes 1048576 | tf_op jit(solution)/shard_map/all_to_all | solution.py:59
  43.6 30.3 %all-to-all-start.1 = ((f32[2,32,16,128]{3,2,0,1:T(8,128)}), f32[2,32,16,128]{3,2,0,1:T(8,128)S(1)}, u32[]{:S(2)}, u32[]{:S(2)}) async-start(f32[2,32,16,128]{3,2,0,1:T(8,128)} %pad_maximum_fusion.1), calls=%async_computation.1 | async-start | bytes 1048576 | tf_op jit(solution)/shard_map/all_to_all | solution.py:63
  83.3 13.2 %all-to-all-start.2 = ((f32[2,8,64,128]{3,2,0,1:T(8,128)}), f32[2,8,64,128]{3,2,0,1:T(8,128)S(1)}, u32[]{:S(2)}, u32[]{:S(2)}) async-start(f32[2,8,64,128]{3,2,0,1:T(8,128)} %pad_maximum_fusion.2), calls=%async_computation.2 | async-start | bytes 1048576 | tf_op jit(solution)/shard_map/all_to_all | solution.py:59
where the time goes:
time: 106 us
  waiting for transfers between devices  34.6 us (33%)
  matrix products  24.5 us (23%)
  starting transfers between devices  20.1 us (19%)
  other arithmetic  14.6 us (14%)
  local copies, waits for them, and re-layouts  10.7 us (10%)
  between operations  1.1 us (1%)
    all_to_all x2, waiting for transfers between devices, regroup_with_gate(): lax.all_to_all(blocks, 'qa', split_axis=1, concat_axis=1, tiled=True)  19.1 us
    all_to_all x1, waiting for transfers between devices, regroup_with_gate(): lax.all_to_all(blocks, 'qb', split_axis=1, concat_axis=1, tiled=True)  15.6 us
    all_to_all x1, starting transfers between devices, regroup_with_gate(): lax.all_to_all(blocks, 'qb', split_axis=1, concat_axis=1, tiled=True)  11.1 us
    all_to_all x2, starting transfers between devices, regroup_with_gate(): lax.all_to_all(blocks, 'qa', split_axis=1, concat_axis=1, tiled=True)  9.08 us
    dot_general x8, matrix products, apply_gate(): lax.dot_general(values, stacked, (((1,), (1,)), ((), ())), precision=lax....  8.76 us
    dot_general x8, matrix products, apply_gate(): lax.dot_general(stacked, values, (((1,), (1,)), ((), ())), precision=lax....  7.85 us
    dot_general x8, matrix products, apply_gate(): lax.dot_general(stacked, values, (((1,), (2,)), ((), ())), precision=lax....  7.84 us
    sub x4, other arithmetic, apply_phase(): state[0] * cosine - state[1] * sine  5.93 us
  transfers between devices with their start and end apart: 3, of which 3 were waited for; matrix products, arithmetic and copies ran while one was open for 4% of the time, Pallas kernels for 0%

commit v1 on v0

--- a/solution.py
+++ b/solution.py
@@ -2,6 +2,12 @@
 import jax.numpy as jnp
 from jax import lax
 from jax.sharding import PartitionSpec as P
+
+
+def swap_blocks(x, mesh_axis, split, join):
+    pieces = jnp.split(x, lax.axis_size(mesh_axis), axis=split)
+    received = lax.all_to_all(jnp.stack(pieces), mesh_axis, 0, 0)
+    return jnp.concatenate(received, axis=join)
 
 
 def apply_gate(state, matrix, where):
@@ -56,7 +62,7 @@
     if which == 0:
         count = lax.axis_size("qa")
         blocks = state.reshape(2, count, cells // (count * width), width)
-        moved = lowest_gate(lax.all_to_all(blocks, "qa", split_axis=1, concat_axis=1, tiled=True))
+        moved = lowest_gate(swap_blocks(blocks, "qa", 1, 1))
     else:
         count = lax.axis_size("qb")
         blocks = state.reshape(2, count, cells // (count * width), width)

time: 106 us -> 115 us (1.085)
  other arithmetic: 14.6 us -> 23 us
    unnamed x0 -> x14, other arithmetic: none -> 8.87 us
    add x0 -> x2, other arithmetic: none -> 3.67 us  [apply_phase(): state[0] * sine + state[1] * cosine]
    sub x4 -> x2, other arithmetic: 5.93 us -> 2.26 us  [apply_phase(): state[0] * cosine - state[1] * sine]
    another operation x3 -> x1, other arithmetic: 2.5 us -> 0.83 us  [apply_phase(): jnp.stack([state[0] * cosine - state[1] * sine, state[0] * sine + state[1...]
    another operation x0 -> x2, other arithmetic: none -> 1.27 us  [swap_blocks(): received = lax.all_to_all(jnp.stack(pieces), mesh_axis, 0, 0)]
  transfers between devices with their start and end apart: 3 -> 3, of which waited for: 3 -> 3; matrix products, arithmetic and copies ran while one was open for 4% -> 3% of each run, Pallas kernels for 0% -> 0%
where the time goes in v1:
time: 115 us; the launch traced here: 114 us
  waiting for transfers between devices  34.7 us (30%)
  matrix products  24.5 us (21%)
  other arithmetic  23 us (20%)
  starting transfers between devices  20.1 us (17%)
  local copies, waits for them, and re-layouts  10.7 us (9%)
    all_to_all x2, waiting for transfers between devices, swap_blocks(): received = lax.all_to_all(jnp.stack(pieces), mesh_axis, 0, 0)  19.1 us
    all_to_all x1, waiting for transfers between devices, regroup_with_gate(): lax.all_to_all(blocks, 'qb', split_axis=1, concat_axis=1, tiled=True)  15.6 us
    all_to_all x1, starting transfers between devices, regroup_with_gate(): lax.all_to_all(blocks, 'qb', split_axis=1, concat_axis=1, tiled=True)  11.1 us
    all_to_all x2, starting transfers between devices, swap_blocks(): received = lax.all_to_all(jnp.stack(pieces), mesh_axis, 0, 0)  9.08 us
    unnamed x14, other arithmetic  8.87 us
    dot_general x8, matrix products, apply_gate(): lax.dot_general(values, stacked, (((1,), (1,)), ((), ())), precision=lax....  8.77 us
    dot_general x8, matrix products, apply_gate(): lax.dot_general(stacked, values, (((1,), (2,)), ((), ())), precision=lax....  7.85 us
    dot_general x8, matrix products, apply_gate(): lax.dot_general(stacked, values, (((1,), (1,)), ((), ())), precision=lax....  7.84 us
  transfers between devices with their start and end apart: 3, of which 3 were waited for; matrix products, arithmetic and copies ran while one was open for 3% of the time, Pallas kernels for 0%

profile of v1, /device:TPU:32, one launch (start us, length us, event | category | flops | bytes accessed | tf_op | source)
XLA Modules:
  0.0 114.1 jit_solution(13731846556905242782)
XLA Ops:
  0.0 2.2 %slice_bitcast_fusion.3 = (f32[128,128]{1,0:T(8,128)S(1)}, f32[128,128]{1,0:T(8,128)S(1)}, f32[128,128]{1,0:T(8,128)S(1)}, f32[128,128]{1,0:T(8,128)S(1)}, f32[1...) fusion(f32[4,6,2,128,128]{4,3,2,1,0:T(8,128)} %param.6), kind=kLoop, calls=%fused_computation.280 | loop fusion | bytes 2490368 | tf_op jit(solution)/shard_map/squeeze | solution.py:16
  2.2 2.1 %slice_bitcast_fusion.21 = (f32[128,128]{1,0:T(8,128)}, f32[128,128]{1,0:T(8,128)}, f32[128,128]{1,0:T(8,128)}, f32[128,128]{1,0:T(8,128)S(1)}, f32[128,128]{1,0...) fusion(f32[4,6,2,128,128]{4,3,2,1,0:T(8,128)} %param.6), kind=kLoop, calls=%fused_computation.298 | loop fusion | bytes 2490368 | tf_op jit(solution)/shard_map/squeeze | solution.py:16
  4.8 1.9 %convolution_bitcast_fusion = f32[1024,256]{0,1:T(8,128)S(1)} fusion(f32[1024,128]{1,0:T(8,128)S(1)} %reshape_reshape.2, f32[128,128]{1,0:T(8,128)} %get-tuple-element.20, f32[128,128]{1,0:T(8,128)} %get-tuple-element.21), kind=kOutput, calls=%fused_computation | convolution fusion | flops 402685952 | bytes 1703936 | tf_op jit(solution)/shard_map/dot_general | solution.py:19
  10.5 1.0 fusion.3
  11.8 1.0 fusion.6
  12.9 1.0 fusion.9
  14.1 1.0 fusion.12
  16.2 1.8 %multiply_add_fusion.1 = (f32[1,8,64,128]{3,2,1,0:T(8,128)S(1)}, f32[1,8,64,128]{3,2,1,0:T(8,128)S(1)}) fusion(f32[1,8,64,128]{3,2,1,0:T(8,128)S(1)} %add.638, f32[1,8,64,128]{3,2,1,0:T(8,128)S(1)} %sub.368, f32[64,128]{1,0:T(8,128)S(1)} %bitcast.643, f32[8,64]{1,0:T(8,128)S(1)} %copy.59, f32[]{:T(128)} %bitcast.105), kind=kLoop, calls=%fused_computation.198 | loop fusion | flops 524288 | bytes 1083396 | tf_op jit(solution)/shard_map/add | solution.py:50
  23.1 5.3 %all-to-all-start = ((f32[8,2,1,64,128]{4,3,1,2,0:T(8,128)}), f32[8,2,1,64,128]{4,3,1,2,0:T(8,128)S(1)}, u32[]{:S(2)}, u32[]{:S(2)}) async-start(f32[8,2,1,64,128]{4,3,1,2,0:T(8,128)} %fusion.136), calls=%async_computation | async-start | bytes 1048576 | tf_op jit(solution)/shard_map/all_to_all | solution.py:9
  28.8 9.7 %all-to-all-done = f32[8,2,1,64,128]{4,3,1,2,0:T(8,128)S(1)} async-done(((f32[8,2,1,64,128]{4,3,1,2,0:T(8,128)}), f32[8,2,1,64,128]{4,3,1,2,0:T(8,128)S(1)}, u32[]{:S(2)}, u32[]{:S(2)}) %all-to-all-start) | async-done | bytes 524320 | tf_op jit(solution)/shard_map/all_to_all | solution.py:9
  38.6 1.0 fusion.160
  39.6 1.0 fusion.15
  40.8 1.0 fusion.18
  41.9 1.0 fusion.21
  43.0 1.0 fusion.24
  45.3 1.7 %fusion.78 = (f32[1,32,16,128]{3,2,0,1:T(8,128)S(1)}, f32[1,32,16,128]{3,2,0,1:T(8,128)S(1)}) fusion(f32[1,32,16,128]{3,2,1,0:T(8,128)S(1)} %add.663, f32[1,32,16,128]{3,2,1,0:T(8,128)S(1)} %sub.381, f32[16,128]{1,0:T(8,128)S(1)} %bitcast.646, f32[32,16]{1,0:T(8,128)S(1)} %copy.69, f32[]{:T(128)} %bitcast.148), kind=kLoop, calls=%fused_computation.183 | loop fusion | flops 524288 | bytes 1058820 | tf_op jit(solution)/shard_map/sub | solution.py:50
  47.8 11.1 %all-to-all-start.1 = ((f32[2,32,16,128]{3,2,0,1:T(8,128)}), f32[2,32,16,128]{3,2,0,1:T(8,128)S(1)}, u32[]{:S(2)}, u32[]{:S(2)}) async-start(f32[2,32,16,128]{3,2,0,1:T(8,128)} %pad_maximum_fusion), calls=%async_computation.1 | async-start | bytes 1048576 | tf_op jit(solution)/shard_map/all_to_all | solution.py:69
  59.1 1.6 %fusion.80 = (f32[256,256]{1,0:T(8,128)S(1)}, f32[256,256]{1,0:T(8,128)S(1)}) fusion(f32[256]{0:T(256)S(1)} %bitcast.649, f32[256]{0:T(256)S(1)} %bitcast.648, f32[]{:T(128)} %bitcast.227), kind=kLoop, calls=%fused_computation.188 | loop fusion | flops 131072 | bytes 526340 | tf_op jit(solution)/shard_map/sin | solution.py:49
  61.4 1.2 %slice_bitcast_fusion.41 = (f32[128,128]{1,0:T(8,128)S(1)}, f32[128,128]{1,0:T(8,128)S(1)}, f32[128,128]{1,0:T(8,128)S(1)}, f32[128,128]{1,0:T(8,128)S(1)}, f32[...) fusion(f32[4,6,2,128,128]{4,3,2,1,0:T(8,128)} %param.6), kind=kLoop, calls=%fused_computation.318 | loop fusion | bytes 1310720 | tf_op jit(solution)/shard_map/squeeze | solution.py:16
  62.6 15.6 %all-to-all-done.1 = f32[2,32,16,128]{3,2,0,1:T(8,128)S(1)} async-done(((f32[2,32,16,128]{3,2,0,1:T(8,128)}), f32[2,32,16,128]{3,2,0,1:T(8,128)S(1)}, u32[]{:S(2)}, u32[]{:S(2)}) %all-to-all-start.1) | async-done | bytes 524320 | tf_op jit(solution)/shard_map/all_to_all | solution.py:69
  78.2 1.0 fusion.161
  80.4 1.0 fusion.33
  81.5 1.0 fusion.36
  82.6 1.0 fusion.39
  84.9 1.9 %multiply_add_fusion = (f32[1,8,64,128]{3,2,1,0:T(8,128)S(1)}, f32[1,8,64,128]{3,2,1,0:T(8,128)S(1)}) fusion(f32[1,8,64,128]{3,2,1,0:T(8,128)S(1)} %add.688, f32[1,8,64,128]{3,2,1,0:T(8,128)S(1)} %sub.394, f32[64,128]{1,0:T(8,128)S(1)} %bitcast.642, f32[8,64]{1,0:T(8,128)S(1)} %copy.76, f32[]{:T(128)} %bitcast.184), kind=kLoop, calls=%fused_computation.190 | loop fusion | flops 524288 | bytes 1083396 | tf_op jit(solution)/shard_map/add | solution.py:50
  91.8 3.8 %all-to-all-start.2 = ((f32[8,2,1,64,128]{4,3,1,2,0:T(8,128)}), f32[8,2,1,64,128]{4,3,1,2,0:T(8,128)S(1)}, u32[]{:S(2)}, u32[]{:S(2)}) async-start(f32[8,2,1,64,128]{4,3,1,2,0:T(8,128)} %fusion.134), calls=%async_computation.2 | async-start | bytes 1048576 | tf_op jit(solution)/shard_map/all_to_all | solution.py:9
  95.7 9.3 %all-to-all-done.2 = f32[8,2,1,64,128]{4,3,1,2,0:T(8,128)S(1)} async-done(((f32[8,2,1,64,128]{4,3,1,2,0:T(8,128)}), f32[8,2,1,64,128]{4,3,1,2,0:T(8,128)S(1)}, u32[]{:S(2)}, u32[]{:S(2)}) %all-to-all-start.2) | async-done | bytes 524320 | tf_op jit(solution)/shard_map/all_to_all | solution.py:9
  105.1 1.0 fusion.162
  107.3 1.0 fusion.48
  108.4 1.0 fusion.51
  109.5 1.0 fusion.54
  112.9 1.3 %maximum_bitcast_fusion.40 = f32[2,65536]{1,0:T(2,128)} fusion(f32[1,1,65536]{2,0,1:T(1,128)S(1)} %get-tuple-element.57, f32[1,1,65536]{2,0,1:T(1,128)S(1)} %get-tuple-element.56), kind=kLoop, calls=%fused_computation.110 | loop fusion | flops 131072 | bytes 1048576 | tf_op jit(solution)/shard_map/reshape | solution.py:92
  (149 shorter events, 25.9 us)
Async XLA Ops:
  0.0 4.3 %copy-start = (f32[2,65536]{1,0:T(2,128)S(1)}, f32[2,65536]{1,0:T(2,128)}, u32[]{:S(2)}) copy-start(f32[2,65536]{1,0:T(2,128)} %param.5) | copy-start | bytes 1572868
  10.3 1.4 %copy-start.7 = (f32[128,128]{1,0:T(8,128)S(1)}, f32[128,128]{1,0:T(8,128)}, u32[]{:S(2)}) copy-start(f32[128,128]{1,0:T(8,128)} %get-tuple-element.14) | copy-start | bytes 196612
  10.3 1.4 %copy-start.8 = (f32[128,128]{1,0:T(8,128)S(1)}, f32[128,128]{1,0:T(8,128)}, u32[]{:S(2)}) copy-start(f32[128,128]{1,0:T(8,128)} %get-tuple-element.15) | copy-start | bytes 196612
  10.3 1.4 %copy-start.9 = (f32[128,128]{1,0:T(8,128)S(1)}, f32[128,128]{1,0:T(8,128)}, u32[]{:S(2)}) copy-start(f32[128,128]{1,0:T(8,128)} %get-tuple-element.18) | copy-start | bytes 196612
  10.4 1.4 %copy-start.10 = (f32[128,128]{1,0:T(8,128)S(1)}, f32[128,128]{1,0:T(8,128)}, u32[]{:S(2)}) copy-start(f32[128,128]{1,0:T(8,128)} %get-tuple-element.19) | copy-start | bytes 196612
  11.5 1.3 %copy-start.3 = (f32[128,128]{1,0:T(8,128)S(1)}, f32[128,128]{1,0:T(8,128)}, u32[]{:S(2)}) copy-start(f32[128,128]{1,0:T(8,128)} %get-tuple-element.26) | copy-start | bytes 196612
  11.5 1.3 %copy-start.4 = (f32[128,128]{1,0:T(8,128)S(1)}, f32[128,128]{1,0:T(8,128)}, u32[]{:S(2)}) copy-start(f32[128,128]{1,0:T(8,128)} %get-tuple-element.27) | copy-start | bytes 196612
  11.5 1.3 %copy-start.5 = (f32[128,128]{1,0:T(8,128)S(1)}, f32[128,128]{1,0:T(8,128)}, u32[]{:S(2)}) copy-start(f32[128,128]{1,0:T(8,128)} %get-tuple-element.28) | copy-start | bytes 196612
  11.5 1.3 %copy-start.6 = (f32[128,128]{1,0:T(8,128)S(1)}, f32[128,128]{1,0:T(8,128)}, u32[]{:S(2)}) copy-start(f32[128,128]{1,0:T(8,128)} %get-tuple-element.29) | copy-start | bytes 196612
  13.9 1.3 %copy-start.12 = (f32[4,256]{1,0:T(4,128)S(1)}, f32[4,256]{1,0:T(4,128)}, u32[]{:S(2)}) copy-start(f32[4,256]{1,0:T(4,128)} %param.8) | copy-start | bytes 12292
  14.0 1.5 %copy-start.13 = (f32[4,256]{1,0:T(4,128)S(1)}, f32[4,256]{1,0:T(4,128)}, u32[]{:S(2)}) copy-start(f32[4,256]{1,0:T(4,128)} %param.7) | copy-start | bytes 12292
  14.0 1.5 %copy-start.11 = (f32[4,1,1]{0,2,1:T(1,128)S(1)}, f32[4,1,1]{0,2,1:T(1,128)}, u32[]{:S(2)}) copy-start(f32[4,1,1]{0,2,1:T(1,128)} %param.9) | copy-start | bytes 52
  18.0 10.7 %copy-start.1 = (f32[128,128]{1,0:T(8,128)S(1)}, f32[128,128]{1,0:T(8,128)}, u32[]{:S(2)}) copy-start(f32[128,128]{1,0:T(8,128)} %get-tuple-element.32) | copy-start | bytes 196612
  18.0 10.7 %copy-start.2 = (f32[128,128]{1,0:T(8,128)S(1)}, f32[128,128]{1,0:T(8,128)}, u32[]{:S(2)}) copy-start(f32[128,128]{1,0:T(8,128)} %get-tuple-element.33) | copy-start | bytes 196612
  23.1 15.4 %all-to-all-start = ((f32[8,2,1,64,128]{4,3,1,2,0:T(8,128)}), f32[8,2,1,64,128]{4,3,1,2,0:T(8,128)S(1)}, u32[]{:S(2)}, u32[]{:S(2)}) async-start(f32[8,2,1,64,128]{4,3,1,2,0:T(8,128)} %fusion.136), calls=%async_computation | async-start | bytes 1048576 | tf_op jit(solution)/shard_map/all_to_all | solution.py:9
  47.8 30.3 %all-to-all-start.1 = ((f32[2,32,16,128]{3,2,0,1:T(8,128)}), f32[2,32,16,128]{3,2,0,1:T(8,128)S(1)}, u32[]{:S(2)}, u32[]{:S(2)}) async-start(f32[2,32,16,128]{3,2,0,1:T(8,128)} %pad_maximum_fusion), calls=%async_computation.1 | async-start | bytes 1048576 | tf_op jit(solution)/shard_map/all_to_all | solution.py:69
  91.8 13.2 %all-to-all-start.2 = ((f32[8,2,1,64,128]{4,3,1,2,0:T(8,128)}), f32[8,2,1,64,128]{4,3,1,2,0:T(8,128)S(1)}, u32[]{:S(2)}, u32[]{:S(2)}) async-start(f32[8,2,1,64,128]{4,3,1,2,0:T(8,128)} %fusion.134), calls=%async_computation.2 | async-start | bytes 1048576 | tf_op jit(solution)/shard_map/all_to_all | solution.py:9
